TPU v7x, 32 devices: a whole 2x2x4 slice. The times are simulated.
32 devices in a mesh: seq: 8 (over z, y), head: 4 (over x, core).
Axes of the slice: x: 2, y: 2, z: 4, core: 2. Of those that a mesh axis runs over, the one named last changes fastest.
Arguments:
- queries: bfloat16 [8192, 32, 128], P('seq', 'head'), may hold values from -0.59765625 to 0.59765625
- keys: bfloat16 [8192, 32, 128], P('seq', 'head'), may hold values from -6 to 6
- values: bfloat16 [8192, 32, 128], P('seq', 'head'), may hold values from -6 to 6
- log_decay: float32 [8192, 32], P('seq', 'head'), may hold values from -0.8 to 0, as said below
- level_weight: float32 [8192, 32, 8], P('seq', 'head'), may hold values from 0.1 to 2
- norm_gain: float32 [32, 128], P('head'), may hold values from 0.25 to 1.75
- out_weight: bfloat16 [4096, 4096], P('head'), may hold values from -0.09375 to 0.09375
Outputs:
- mixed: bfloat16 [8192, 4096], P(('seq', 'head'))
Inputs may be any that keep to these rules, and one draw needn't show every extreme that they name: `log_decay`: negative logarithms of decay factors.
All inputs are finite; a program needn't handle non-finite values.
Results may differ from a plain program's by a relative error of at most 0.023.
Values may be sent and summed in bfloat16 or wider, within the bound.
A program may use at most 128 MiB of HBM per device.

v0:
```python
import jax
import jax.numpy as jnp
import numpy as np
from jax import lax
from jax.sharding import PartitionSpec as P

SPAN = 64


def span_terms(query_blocks, key_blocks, value_blocks, inner):
    size = inner.shape[1]
    scores = jnp.einsum(
        "cthd,cshd->chts", query_blocks, key_blocks, preferred_element_type=jnp.float32
    )
    leading = jnp.transpose(inner, (0, 2, 1))
    causal = np.tril(np.ones((size, size), dtype=bool))
    spread = jnp.where(causal, leading[:, :, :, None] - leading[:, :, None, :], 0.0)
    weight = jnp.where(causal, jnp.exp(spread), 0.0)
    probs = (scores * weight).astype(jnp.bfloat16)
    within = jnp.einsum("chts,cshe->cthe", probs, value_blocks, preferred_element_type=jnp.float32)
    scaled = (jnp.exp(inner[:, -1:, :] - inner)[:, :, :, None] * key_blocks).astype(jnp.bfloat16)
    states = jnp.einsum("cshd,cshe->chde", scaled, value_blocks, preferred_element_type=jnp.float32)
    return (within, states)


def local_levels(query_blocks, inner, states, totals, before, weights):
    count = states.shape[0]
    depth = count.bit_length() - 1
    output = jnp.zeros(query_blocks.shape, jnp.float32)
    blocks = states
    block_total = totals
    span_ids = np.arange(count)
    for level_now in range(1, depth + 1):
        shift_by = level_now - 1
        present = (span_ids >> shift_by & 1).astype(np.float32)
        source = np.maximum((span_ids >> shift_by) - 1, 0)
        middle = span_ids >> shift_by << shift_by
        picked = blocks[source].astype(jnp.bfloat16)
        readout = jnp.einsum(
            "cthd,chde->cthe", query_blocks, picked, preferred_element_type=jnp.float32
        )
        factor = (
            jnp.exp((before - before[middle])[:, None, :] + inner)
            * weights[:, :, :, level_now]
            * present[:, None, None]
        )
        output = output + factor[:, :, :, None] * readout
        blocks = jnp.exp(block_total[1::2])[:, :, None, None] * blocks[0::2] + blocks[1::2]
        block_total = block_total[0::2] + block_total[1::2]
    return (output, blocks[0], block_total[0])


def body(queries, keys, values, log_decay, level_weight, norm_gain, out_weight):
    row_count, head_count, head_width = queries.shape
    span_count = row_count // SPAN
    local_depth = span_count.bit_length() - 1
    seq_bits = lax.axis_size("seq").bit_length() - 1
    position = lax.axis_index("seq")
    shaped = (span_count, SPAN, head_count, head_width)
    query_blocks = queries.reshape(shaped)
    key_blocks = keys.reshape(shaped)
    value_blocks = values.reshape(shaped)
    weights = level_weight.reshape(span_count, SPAN, head_count, level_weight.shape[2])
    inner = jnp.cumsum(log_decay.reshape(span_count, SPAN, head_count), axis=1)
    totals = inner[:, -1, :]
    before = jnp.cumsum(totals, axis=0) - totals
    within, states = span_terms(query_blocks, key_blocks, value_blocks, inner)
    output = within * weights[:, :, :, 0:1]
    nearby, summary, summary_total = local_levels(
        query_blocks, inner, states, totals, before, weights
    )
    output = output + nearby
    all_totals = lax.all_gather(summary_total[None], "seq", axis=0, tiled=True)
    device_before = jnp.cumsum(all_totals, axis=0) - all_totals
    own_before = lax.dynamic_index_in_dim(device_before, position, 0, keepdims=False)
    bit_range = jnp.arange(seq_bits, dtype=jnp.int32)
    middles = position >> bit_range << bit_range
    middle_before = jnp.take(device_before, middles, axis=0)
    initial = jnp.zeros((seq_bits,) + summary.shape, jnp.float32)
    piece = lax.all_gather(summary[None].astype(jnp.bfloat16), "seq", axis=0, tiled=True).astype(
        jnp.float32
    )
    piece_rows = piece.shape[0]
    sources = jnp.arange(piece_rows, dtype=jnp.int32)
    mixed_bits = sources ^ position
    level_of = jnp.zeros((piece_rows,), jnp.int32)
    for bit_now in range(1, seq_bits):
        level_of = level_of + (mixed_bits >> bit_now > 0).astype(jnp.int32)
    valid = sources < position
    select = (level_of[:, None] == bit_range[None, :]) & valid[:, None]
    source_end = device_before + all_totals
    gap = middle_before[None, :, :] - source_end[:, None, :]
    gap = jnp.where(select[:, :, None], gap, 0.0)
    factor = select.astype(jnp.float32)[:, :, None] * jnp.exp(gap)
    far_states = initial + jnp.einsum(
        "mbh,mhde->bhde", factor, piece, precision=lax.Precision.HIGHEST
    )
    far_offset = own_before[None, :] - middle_before
    far_flag = (position >> bit_range & 1).astype(jnp.float32)
    far_cast = far_states.astype(jnp.bfloat16)
    far_read = jnp.einsum(
        "cthd,bhde->ctbhe", query_blocks, far_cast, preferred_element_type=jnp.float32
    )
    far_weight = jnp.transpose(weights[:, :, :, local_depth + 1 :], (0, 1, 3, 2))
    exponent = far_offset[None, None, :, :] + (before[:, None, :] + inner)[:, :, None, :]
    far_factor = jnp.exp(exponent) * far_flag[None, None, :, None] * far_weight
    output = output + jnp.sum(far_factor[:, :, :, :, None] * far_read, axis=2)
    attention = output.reshape(row_count, head_count, head_width)
    mean_square = jnp.mean(attention * attention, axis=-1, keepdims=True)
    normed = (attention * lax.rsqrt(mean_square + 1e-06) * norm_gain[None]).astype(jnp.bfloat16)
    normed = normed.reshape(row_count, head_count * head_width)
    return lax.psum_scatter(
        jnp.dot(normed, out_weight, preferred_element_type=jnp.float32).astype(jnp.bfloat16),
        "head",
        scatter_dimension=0,
        tiled=True,
    )


def solution(mesh):
    return jax.shard_map(
        body,
        mesh=mesh,
        in_specs=(
            P("seq", "head", None),
            P("seq", "head", None),
            P("seq", "head", None),
            P("seq", "head"),
            P("seq", "head", None),
            P("head", None),
            P("head", None),
        ),
        out_specs=P(("seq", "head"), None),
        check_vma=False,
    )
```

profile of v0, /device:TPU:0, one launch (start us, length us, event | category | flops | bytes accessed | tf_op | source)
XLA Modules:
  0.0 234.9 jit_solution(17910996043760039328)
XLA Ops:
  6.5 1.0 reshape.266
  7.5 0.3 copy.245
  7.8 6.3 %fusion.91 = f32[16,64,8]{2,0,1:T(8,128)S(1)} fusion(f32[16,64,8]{2,0,1:T(8,128)S(1)} %copy.245), kind=kOutput, calls=%fused_computation.141 | output fusion | flops 516096 | bytes 65536 | tf_op jit(solution)/shard_map/jit(cumsum)/reduce_window_sum | solution.py:64
  14.3 0.1 slice.86
  14.3 0.1 slice.82
  14.4 0.1 slice.91
  14.5 0.1 slice.87
  14.6 0.1 slice.95
  14.7 0.1 slice.92
  15.0 0.1 copy.273
  15.0 0.2 exponential_reduce_fusion
  15.2 0.1 copy.279
  15.3 0.6 gather_fusion
  16.0 0.9 broadcast_add_fusion
  16.9 0.2 copy.259
  17.2 5.7 %fusion.16 = f32[16,8,128,128]{3,2,1,0:T(8,128)S(1)} fusion(f32[16,64,8]{1,2,0:T(8,128)S(1)} %copy.259, bf16[16,64,8,128]{3,2,1,0:T(8,128)(2,1)S(1)} %bitcast.163, bf16[16,64,8,128]{3,2,1,0:T(8,128)(2,1)} %bitcast.171), kind=kOutput, calls=%fused_computation.37 | convolution fusion | flops 271581184 | bytes 12615680 | tf_op jit(solution)/shard_map/cshd,cshe->chde/dot_general | solution.py:22
  22.9 0.5 slice_add_fusion
  23.4 2.7 %copy-done.3 = f32[16,8,128,128]{3,2,1,0:T(8,128)} copy-done((f32[16,8,128,128]{3,2,1,0:T(8,128)}, f32[16,8,128,128]{3,2,1,0:T(8,128)S(1)}, u32[]{:S(2)}) %copy-start.3) | copy-done | bytes 8388632
  26.1 0.3 slice_add_fusion.1
  26.4 0.2 slice_add_fusion.2
  26.6 1.5 copy-done.4
  28.1 0.7 copy-done.5
  28.8 0.9 fusion.43
  29.9 22.4 %all-gather = f32[8,1,8]{2,1,0:T(1,128)S(1)} all-gather(f32[1,1,8]{2,1,0:T(1,128)S(1)} %bitcast.182), channel_id=1, replica_groups=mesh['seq'=8,'head'=4] {'seq'}, dimensions={0}, use_global_device_ids=true | all-gather | bytes 288 | tf_op jit(solution)/shard_map/all_gather | solution.py:73
  52.2 0.7 copy.285
  52.9 0.6 gather_fusion.8
  53.5 0.7 copy.281
  54.2 0.7 copy.284
  54.9 0.6 gather_fusion.6
  55.5 0.6 gather_fusion.4
  56.2 0.6 gather_fusion.2
  56.9 0.7 copy.276
  57.6 0.7 copy.270
  58.3 1.3 copy.246
  59.5 0.9 reshape.268
  60.5 1.0 slice_bitcast_fusion.1
  61.5 1.1 copy.305
  62.6 1.0 copy.304
  63.6 1.1 copy.303
  64.7 1.0 copy.306
  65.7 3.3 %fusion.47 = (f32[16,64,8]{2,0,1:T(8,128)}, f32[16,64,8]{2,0,1:T(8,128)}, f32[16,64,8]{2,0,1:T(8,128)}, f32[16,64,8]{2,0,1:T(8,128)}) fusion(f32[16,64,8,1]{2,0,1,3:T(8,128)} %copy.303, f32[16,64,8]{2,0,1:T(8,128)} %copy-done.9, f32[16]{0:T(128)} %constant.95, f32[16,8]{1,0:T(8,128)S(1)} %copy.255, f32[16]{0:T(128)} %constant.98, ...), kind=kLoop, calls=%fused_computation.67 | loop fusion | flops 98304 | bytes 297216 | tf_op jit(solution)/shard_map/mul | solution.py:47
  69.0 1.3 copy.257
  70.3 1.3 copy.266
  71.5 1.3 copy.272
  72.8 1.3 copy.278
  74.1 1.9 copy.283
  75.9 0.7 pad_clamp_fusion.7
  76.6 6.3 %gather_fusion.1 = bf16[16,8,128,128]{3,2,1,0:T(8,128)(2,1)} fusion(f32[16,8,128,128]{3,2,1,0:T(8,128)} %copy-done.3, s32[1024]{0:T(1024)S(1)} %pad_clamp_fusion.7), kind=kCustom, calls=%fused_computation.1 | custom fusion | bytes 8388672 | tf_op jit(solution)/shard_map/gather | solution.py:38
  82.9 5.1 %gather_fusion.3 = bf16[16,8,128,128]{3,2,1,0:T(8,128)(2,1)} fusion(f32[8,8,128,128]{3,2,1,0:T(8,128)} %copy-done.4, s32[1024]{0:T(1024)S(1)} %pad_clamp_fusion.5), kind=kCustom, calls=%fused_computation.3 | custom fusion | bytes 8388672 | tf_op jit(solution)/shard_map/gather | solution.py:38
  88.1 4.5 %gather_fusion.5 = bf16[16,8,128,128]{3,2,1,0:T(8,128)(2,1)} fusion(f32[4,8,128,128]{3,2,1,0:T(8,128)} %copy-done.5, s32[1024]{0:T(1024)S(1)} %pad_clamp_fusion.3), kind=kCustom, calls=%fused_computation.5 | custom fusion | bytes 8388672 | tf_op jit(solution)/shard_map/gather | solution.py:38
  92.6 2.9 %gather_fusion.7 = bf16[16,8,128,128]{3,2,1,0:T(8,128)(2,1)} fusion(f32[2,8,128,128]{3,2,1,0:T(8,128)S(1)} %slice_add_fusion.2, s32[1024]{0:T(1024)S(1)} %pad_clamp_fusion.1), kind=kCustom, calls=%fused_computation.7 | custom fusion | bytes 8388672 | tf_op jit(solution)/shard_map/gather | solution.py:38
  95.5 1.0 fusion.60
  96.6 6.2 %fusion.14 = f32[16,8,128,64]{2,3,1,0:T(8,128)} fusion(bf16[16,8,128,128]{3,2,1,0:T(8,128)(2,1)} %gather_fusion.1, bf16[16,64,8,128]{3,2,1,0:T(8,128)(2,1)} %bitcast.164), kind=kOutput, calls=%fused_computation.33 | convolution fusion | flops 268435456 | bytes 10485760 | tf_op jit(solution)/shard_map/cthd,chde->cthe/dot_general | solution.py:39
  102.8 3.2 %fusion.12 = f32[16,8,128,64]{2,3,1,0:T(8,128)} fusion(bf16[16,8,128,128]{3,2,1,0:T(8,128)(2,1)S(1)} %copy-done.6, bf16[16,64,8,128]{3,2,1,0:T(8,128)(2,1)S(1)} %bitcast.167), kind=kOutput, calls=%fused_computation.30 | convolution fusion | flops 268435456 | bytes 10485760 | tf_op jit(solution)/shard_map/cthd,chde->cthe/dot_general | solution.py:39
  106.0 3.2 %fusion.10 = f32[16,8,128,64]{2,3,1,0:T(8,128)} fusion(bf16[16,8,128,128]{3,2,1,0:T(8,128)(2,1)S(1)} %copy-done.7, bf16[16,64,8,128]{3,2,1,0:T(8,128)(2,1)S(1)} %bitcast.168), kind=kOutput, calls=%fused_computation.28 | convolution fusion | flops 268435456 | bytes 10485760 | tf_op jit(solution)/shard_map/cthd,chde->cthe/dot_general | solution.py:39
  109.2 3.2 %fusion.8 = f32[16,8,128,64]{2,3,1,0:T(8,128)} fusion(bf16[16,8,128,128]{3,2,1,0:T(8,128)(2,1)S(1)} %copy-done.8, bf16[16,64,8,128]{3,2,1,0:T(8,128)(2,1)S(1)} %bitcast.169), kind=kOutput, calls=%fused_computation.26 | convolution fusion | flops 268435456 | bytes 10485760 | tf_op jit(solution)/shard_map/cthd,chde->cthe/dot_general | solution.py:39
  112.4 4.4 %fusion.30 = bf16[3,8,128,128,1]{3,0,2,1,4:T(4,128)(2,1)S(1)} fusion(bf16[8,8,128,128]{3,2,1,0:T(8,128)(2,1)} %all-gather.3.cloned.1.call-done, f32[8,8]{0,1:T(8,128)S(1)} %copy-done.11, f32[3,8]{0,1:T(8,128)S(1)} %copy-done.12, f32[8,3]{0,1:T(4,128)S(1)} %get-tuple-element.9, pred[8,3]{0,1:T(4,128)(4,1)S(1)} %get-tuple-element.10), kind=kOutput, calls=%fused_computation.49 | convolution fusion | flops 38142528 | bytes 2884056 | tf_op jit(solution)/shard_map/mbh,mhde->bhde/dot_general | solution.py:95
  116.8 7.6 %fusion = f32[16,64,8,128]{3,1,0,2:T(8,128)} fusion(f32[16,64,3,8]{1,0,2,3:T(8,128)S(1)} %fusion.60, bf16[16,64,8,128,1]{3,2,1,0,4:T(8,128)(2,1)} %bitcast.165, bf16[3,8,128,128,1]{3,0,2,1,4:T(4,128)(2,1)S(1)} %fusion.30), kind=kOutput, calls=%fused_computation.10 | convolution fusion | flops 810549248 | bytes 7176192 | tf_op jit(solution)/shard_map/cthd,bhde->ctbhe/dot_general | solution.py:101
  124.4 13.0 %multiply_reduce_fusion = (f32[16,64,8]{1,2,0:T(8,128)S(1)}, f32[16,64,8,128]{3,1,2,0:T(8,128)}) fusion(f32[16,64,8,128]{3,1,0,2:T(8,128)} %fusion, f32[16,8,128,64]{2,3,1,0:T(8,128)} %fusion.8, f32[16,64,8]{1,2,0:T(8,128)S(1)} %copy.278, f32[16,8,128,64]{2,3,1,0:T(8,128)} %fusion.10, f32[16,64,8]{1,2,0:T(8,128)S(1)} %copy.272, ...), kind=kOutput, calls=%fused_computation.25 | convolution fusion | flops 283631616 | bytes 31690752 | tf_op jit(solution)/shard_map/chts,cshe->cthe/dot_general | solution.py:20
  137.4 0.2 copy.300
  137.6 5.5 %copy.290 = f32[16,64,8,128]{3,2,1,0:T(8,128)S(1)} copy(f32[16,64,8,128]{3,1,2,0:T(8,128)} %get-tuple-element.38) | data formatting | bytes 8388608 | tf_op jit(solution)/shard_map/add | solution.py:107
  143.1 1.1 mul.259
  144.3 14.6 %convolution_convert_fusion = bf16[1024,4096]{1,0:T(8,128)(2,1)} fusion(bf16[1024,4096]{1,0:T(8,128)(2,1)} %param.34, f32[128,8,8,128]{3,2,1,0:T(8,128)S(1)} %bitcast.173, f32[128,8,8,128]{3,2,1,0:T(8,128)S(1)} %bitcast.174, f32[1024]{0:T(1024)S(1)} %bitcast.183), kind=kOutput, calls=%fused_computation.11 | convolution fusion | flops 8597274624 | bytes 25169920 | tf_op jit(solution)/shard_map/dot_general | solution.py:113
  158.9 69.1 %reduce-scatter.2.cloned.1.call-done = bf16[256,4096]{1,0:T(8,128)(2,1)} async-done(((bf16[1024,4096]{1,0:T(8,128)(2,1)}), bf16[256,4096]{1,0:T(8,128)(2,1)}) %reduce-scatter.2.cloned.1.call-update) | async-done | bytes 2097168 | tf_op jit(solution)/shard_map/reduce_scatter | solution.py:112
  (84 shorter events, 1.2 us)
Async XLA Ops:
  6.5 10.6 %copy-start = (bf16[1024,8,128]{2,1,0:T(8,128)(2,1)S(1)}, bf16[1024,8,128]{2,1,0:T(8,128)(2,1)}, u32[]{:S(2)}) copy-start(bf16[1024,8,128]{2,1,0:T(8,128)(2,1)} %param.30) | copy-start | bytes 6291460
  6.5 105.8 %all-gather.3.cloned.1.call-start = ((), (), s32[]{:S(2)}) async-start(), calls=%async_computation.1 | async-start | bytes 2359296 | tf_op jit(solution)/shard_map/all_gather | solution.py:80
  14.2 8.7 %copy-start.9 = (f32[16,64,8]{2,0,1:T(8,128)}, f32[16,64,8]{2,0,1:T(8,128)S(1)}, u32[]{:S(2)}) copy-start(f32[16,64,8]{2,0,1:T(8,128)S(1)} %fusion.91) | copy-start | bytes 98308
  22.9 3.2 %copy-start.3 = (f32[16,8,128,128]{3,2,1,0:T(8,128)}, f32[16,8,128,128]{3,2,1,0:T(8,128)S(1)}, u32[]{:S(2)}) copy-start(f32[16,8,128,128]{3,2,1,0:T(8,128)S(1)} %fusion.16) | copy-start | bytes 25165828
  26.1 2.0 copy-start.4
  26.1 3.7 %copy-start.19 = (s32[16]{0:T(128)S(1)}, s32[16]{0:T(128)}, u32[]{:S(2)}) copy-start(s32[16]{0:T(128)} %constant.106) | copy-start | bytes 196
  26.1 3.7 %copy-start.18 = (s32[16]{0:T(128)S(1)}, s32[16]{0:T(128)}, u32[]{:S(2)}) copy-start(s32[16]{0:T(128)} %constant.108) | copy-start | bytes 196
  26.1 3.7 %copy-start.17 = (s32[16]{0:T(128)S(1)}, s32[16]{0:T(128)}, u32[]{:S(2)}) copy-start(s32[16]{0:T(128)} %constant.110) | copy-start | bytes 196
  26.4 2.4 %copy-start.5 = (f32[4,8,128,128]{3,2,1,0:T(8,128)}, f32[4,8,128,128]{3,2,1,0:T(8,128)S(1)}, u32[]{:S(2)}) copy-start(f32[4,8,128,128]{3,2,1,0:T(8,128)S(1)} %slice_add_fusion.1) | copy-start | bytes 6291460
  26.4 33.1 %copy-start.10 = (f32[1024,8,8]{0,2,1:T(8,128)S(1)}, f32[1024,8,8]{0,2,1:T(8,128)}, u32[]{:S(2)}) copy-start(f32[1024,8,8]{0,2,1:T(8,128)} %param.32) | copy-start | bytes 786436
  29.7 198.4 %reduce-scatter.2.cloned.1.call-start = ((), (), s32[]{:S(2)}) async-start(), calls=%async_computation.2 | async-start | bytes 10485760 | tf_op jit(solution)/shard_map/reduce_scatter | solution.py:112
  76.6 6.3 %copy-start.16 = (s32[16]{0:T(128)S(1)}, s32[16]{0:T(128)}, u32[]{:S(2)}) copy-start(s32[16]{0:T(128)} %constant.107) | copy-start | bytes 196
  82.9 5.1 %copy-start.15 = (s32[16]{0:T(128)S(1)}, s32[16]{0:T(128)}, u32[]{:S(2)}) copy-start(s32[16]{0:T(128)} %constant.109) | copy-start | bytes 196
  92.6 2.9 %copy-start.13 = (f32[3,8]{0,1:T(8,128)S(1)}, f32[3,8]{0,1:T(8,128)}, u32[]{:S(2)}) copy-start(f32[3,8]{0,1:T(8,128)} %copy.281) | copy-start | bytes 292
  96.6 6.2 %copy-start.2 = (bf16[1024,8,128]{2,1,0:T(8,128)(2,1)S(1)}, bf16[1024,8,128]{2,1,0:T(8,128)(2,1)}, u32[]{:S(2)}) copy-start(bf16[1024,8,128]{2,1,0:T(8,128)(2,1)} %param.28) | copy-start | bytes 6291460
  96.6 6.2 %copy-start.6 = (bf16[16,8,128,128]{3,2,1,0:T(8,128)(2,1)S(1)}, bf16[16,8,128,128]{3,2,1,0:T(8,128)(2,1)}, u32[]{:S(2)}) copy-start(bf16[16,8,128,128]{3,2,1,0:T(8,128)(2,1)} %gather_fusion.3) | copy-start | bytes 12582916
  102.8 3.2 %copy-start.7 = (bf16[16,8,128,128]{3,2,1,0:T(8,128)(2,1)S(1)}, bf16[16,8,128,128]{3,2,1,0:T(8,128)(2,1)}, u32[]{:S(2)}) copy-start(bf16[16,8,128,128]{3,2,1,0:T(8,128)(2,1)} %gather_fusion.5) | copy-start | bytes 12582916
  106.0 3.2 %copy-start.8 = (bf16[16,8,128,128]{3,2,1,0:T(8,128)(2,1)S(1)}, bf16[16,8,128,128]{3,2,1,0:T(8,128)(2,1)}, u32[]{:S(2)}) copy-start(bf16[16,8,128,128]{3,2,1,0:T(8,128)(2,1)} %gather_fusion.7) | copy-start | bytes 12582916
  109.2 3.2 %copy-start.11 = (f32[8,8]{0,1:T(8,128)S(1)}, f32[8,8]{0,1:T(8,128)}, u32[]{:S(2)}) copy-start(f32[8,8]{0,1:T(8,128)} %copy.285) | copy-start | bytes 772
  109.2 3.2 %copy-start.12 = (f32[3,8]{0,1:T(8,128)S(1)}, f32[3,8]{0,1:T(8,128)}, u32[]{:S(2)}) copy-start(f32[3,8]{0,1:T(8,128)} %copy.284) | copy-start | bytes 292
  116.8 7.6 %copy-start.14 = (pred[64,64]{1,0:T(32,128)(4,1)S(1)}, pred[64,64]{1,0:T(32,128)(4,1)}, u32[]{:S(2)}) copy-start(pred[64,64]{1,0:T(32,128)(4,1)} %constant.82.clone) | copy-start | bytes 12292
  143.1 1.2 copy-start.20
  158.9 69.1 %copy-start.1 = (bf16[1024,8,128]{2,1,0:T(8,128)(2,1)S(1)}, bf16[1024,8,128]{2,1,0:T(8,128)(2,1)}, u32[]{:S(2)}) copy-start(bf16[1024,8,128]{2,1,0:T(8,128)(2,1)} %param.30) | copy-start | bytes 6291460
Sparse Core Ops, SparseCore 0:
  29.8 52.1 all-gather.2
  159.1 68.9 reduce-scatter.1
where the time goes:
time: 236 us; the launch traced here: 235 us
  waiting for transfers between devices  69.1 us (29%)
  matrix products  61.1 us (26%)
  local copies, waits for them, and re-layouts  54.1 us (23%)
  blocking collectives  22.4 us (9%)
  other arithmetic  14.4 us (6%)
  between operations  13.8 us (6%)
    reduce_scatter x1, waiting for transfers between devices, body(): lax.psum_scatter(jnp.dot(normed, out_weight, preferred_element_type=jnp.f...  69.1 us
    all_gather x1, blocking collectives, body(): all_totals = lax.all_gather(summary_total[None], 'seq', axis=0, tiled=True)  22.4 us
    gather x4, local copies, waits for them, and re-layouts, local_levels(): picked = blocks[source].astype(jnp.bfloat16)  18.8 us
    dot_general x4, matrix products, local_levels(): jnp.einsum('cthd,chde->cthe', query_blocks, picked, preferred_element_typ...  15.8 us
    dot_general x1, matrix products, body(): jnp.dot(normed, out_weight, preferred_element_type=jnp.float32)  14.6 us
    dot_general x1, matrix products, span_terms(): jnp.einsum('chts,cshe->cthe', probs, value_blocks, preferred_element_type...  13 us
    unnamed x47, local copies, waits for them, and re-layouts  9.34 us
    dot_general x1, matrix products, body(): jnp.einsum('cthd,bhde->ctbhe', query_blocks, far_cast, preferred_element_...  7.58 us
  transfers between devices with their start and end apart: 2, of which 1 were waited for; matrix products, arithmetic and copies ran while one was open for 26% of the time, Pallas kernels for 0%

commit v1 on v0

v1 whole, which is shorter than its diff:
```python
import functools

import jax
import jax.numpy as jnp
from jax import lax
from jax.experimental import pallas as pl
from jax.experimental.pallas import tpu as pltpu
from jax.sharding import PartitionSpec as P

SPAN = 64
QUAD = 4 * SPAN
PIECES = 4
F32 = jnp.float32
BF16 = jnp.bfloat16
HIGH = lax.Precision.HIGHEST
MESH = pl.DeviceIdType.MESH


def kernel(
    chips, bits, heads, levels, width,
    q_hbm, k_hbm, v_hbm, w_hbm, ld_ref, ldt_ref, lw_ref, gain_ref, out_ref,
    q, k, v, w, cum, cumt, tots, state, lev, attn, normed,
    summary, sum_send, sum_recv, tot_send, tot_recv, far,
    core_send, core_recv, x_send, x_recv, acc,
    in_sem, ss_sem, sr_sem, ts_sem, tr_sem, cs_sem, cr_sem, xs_sem, xr_sem,
):
    rows_all = q.shape[0]
    quads = rows_all // QUAD
    block = out_ref.shape[0]
    group = 2 * block
    piece_cols = out_ref.shape[1] // PIECES
    position = lax.axis_index("seq")
    head_id = lax.axis_index("head")
    chip = head_id // 2
    core = head_id % 2
    other_core = chip * 2 + (1 - core)

    loads = [
        pltpu.make_async_copy(src, dst, in_sem.at[n])
        for n, (src, dst) in enumerate(((k_hbm, k), (v_hbm, v), (q_hbm, q), (w_hbm, w)))
    ]
    for load in loads:
        load.start()

    bit_of = [(position // (1 << b)) % 2 for b in range(bits)]
    partner_of = [position + (1 - 2 * bit_of[b]) * (1 << b) for b in range(bits)]
    chip_of = [(chip + 1 + i) % chips for i in range(chips)]

    barrier = pltpu.get_barrier_semaphore()
    for b in range(bits):
        pl.semaphore_signal(barrier, inc=1, device_id={"seq": partner_of[b]}, device_id_type=MESH)
    pl.semaphore_signal(barrier, inc=1, device_id={"head": other_core}, device_id_type=MESH)
    for i in range(chips - 1):
        pl.semaphore_signal(
            barrier, inc=1, device_id={"head": chip_of[i] * 2 + core}, device_id_type=MESH
        )
    pl.semaphore_wait(barrier, bits + chips)

    row_id = lax.broadcasted_iota(jnp.int32, (QUAD, QUAD), 0)
    col_id = lax.broadcasted_iota(jnp.int32, (QUAD, QUAD), 1)

    def head_cols(h):
        return slice(h * width, (h + 1) * width)

    def quad_rows(c):
        return pl.ds(pl.multiple_of(c * QUAD, QUAD), QUAD)

    loads[0].wait()
    loads[1].wait()

    @pl.loop(0, quads)
    def _(c):
        rows = quad_rows(c)
        lower = (row_id >= col_id).astype(F32)
        upper = (row_id <= col_id).astype(F32)
        cq = jnp.dot(lower, ld_ref[rows, :], precision=HIGH, preferred_element_type=F32)
        cum[rows, :] = cq
        cumt[c] = jnp.dot(ldt_ref[c], upper, precision=HIGH, preferred_element_type=F32)
        last = cq[QUAD - 1 : QUAD, :]
        tots[c] = jnp.broadcast_to(last, (8, 128))
        decay = jnp.exp(last - cq)
        for h in range(heads):
            hs = head_cols(h)
            scaled = (k[rows, hs].astype(F32) * decay[:, h : h + 1]).astype(BF16)
            state[c, h] = lax.dot_general(
                scaled, v[rows, hs], (((0,), (0,)), ((), ())), preferred_element_type=F32
            )

    t = [tots[c][0:1, :] for c in range(quads)]
    e1, e3, e23 = jnp.exp(t[1]), jnp.exp(t[3]), jnp.exp(t[2] + t[3])
    total = t[0] + t[1] + t[2] + t[3]
    offset = jnp.zeros_like(total)
    before = [jnp.zeros_like(total), t[0], t[0] + t[1], t[0] + t[1] + t[2]]
    nothing = jnp.zeros((width, width), BF16)
    for h in range(heads):
        s0, s2 = state[0, h], state[2, h]
        low = e1[:, h : h + 1] * s0 + state[1, h]
        whole = e23[:, h : h + 1] * low + e3[:, h : h + 1] * s2 + state[3, h]
        summary[h] = whole
        sum_send[0, h] = whole.astype(BF16)
        low_b = low.astype(BF16)
        lev[0, h, :, :width] = nothing
        lev[0, h, :, width:] = nothing
        lev[1, h, :, :width] = s0.astype(BF16)
        lev[1, h, :, width:] = nothing
        lev[2, h, :, :width] = nothing
        lev[2, h, :, width:] = low_b
        lev[3, h, :, :width] = s2.astype(BF16)
        lev[3, h, :, width:] = low_b
    tot_send[0] = jnp.broadcast_to(total, (8, 128))

    def exchange(b):
        return (
            pltpu.make_async_remote_copy(
                sum_send.at[b], sum_recv.at[b], ss_sem.at[b], sr_sem.at[b],
                device_id={"seq": partner_of[b]}, device_id_type=MESH,
            ),
            pltpu.make_async_remote_copy(
                tot_send.at[b], tot_recv.at[b], ts_sem.at[b], tr_sem.at[b],
                device_id={"seq": partner_of[b]}, device_id_type=MESH,
            ),
        )

    for copy in exchange(0):
        copy.start()

    loads[2].wait()

    def local_quad(c):
        rows = quad_rows(c)
        cq = cum[rows, :]
        ecq = jnp.exp(cq)
        ct = cumt[c]
        lwq = lw_ref[rows, :]
        is_last = (c == quads - 1).astype(F32)
        g4 = is_last * jnp.exp(t[2]) + (1.0 - is_last)
        causal = row_id >= col_id
        same = (row_id // SPAN) == (col_id // SPAN)
        near = (row_id // (2 * SPAN)) == (col_id // (2 * SPAN))
        for h in range(heads):
            hs = head_cols(h)
            at = h * levels
            qh = q[rows, hs]
            s = lax.dot_general(
                qh, k[rows, hs], (((1,), (1,)), ((), ())), preferred_element_type=F32
            )
            spread = jnp.where(causal, cq[:, h : h + 1] - ct[h : h + 1, :], -1e30)
            weight = jnp.where(
                same,
                lwq[:, at : at + 1],
                jnp.where(near, lwq[:, at + 1 : at + 2], lwq[:, at + 2 : at + 3]),
            )
            probs = (s * jnp.exp(spread) * weight).astype(BF16)
            o = jnp.dot(probs, v[rows, hs], preferred_element_type=F32)
            read = jnp.dot(qh, lev[c, h], preferred_element_type=F32)
            col = ecq[:, h : h + 1]
            o = o + (col * lwq[:, at + 3 : at + 4]) * read[:, :width]
            o = o + (col * lwq[:, at + 4 : at + 5] * g4[:, h : h + 1]) * read[:, width:]
            attn[rows, hs] = o

    far_gain = []
    for b in range(bits):
        first, last = b * quads // bits, (b + 1) * quads // bits

        @pl.loop(first, last)
        def _(c):
            local_quad(c)

        for copy in exchange(b):
            copy.wait()
        flag = bit_of[b].astype(F32)
        other = tot_recv[b][0:1, :]
        far_gain.append(flag * jnp.exp(offset))
        mine_by = flag + (1.0 - flag) * jnp.exp(other)
        other_by = flag * jnp.exp(total) + (1.0 - flag)
        for h in range(heads):
            got = sum_recv[b, h]
            far[h, :, b * width : (b + 1) * width] = got
            if b < bits - 1:
                joint = (
                    mine_by[:, h : h + 1] * summary[h]
                    + other_by[:, h : h + 1] * got.astype(F32)
                )
                summary[h] = joint
                sum_send[b + 1, h] = joint.astype(BF16)
        offset = offset + flag * other
        total = total + other
        if b < bits - 1:
            tot_send[b + 1] = jnp.broadcast_to(total, (8, 128))
            for copy in exchange(b + 1):
                copy.start()

    loads[3].wait()

    def finish_quad(c, at_row):
        rows = quad_rows(c)
        ecq = jnp.exp(cum[rows, :])
        lwq = lw_ref[rows, :]
        lead = jnp.zeros_like(before[0])
        for n in range(1, quads):
            lead = lead + (c == n).astype(F32) * before[n]
        lead = jnp.exp(lead)
        for h in range(heads):
            hs = head_cols(h)
            read = jnp.dot(q[rows, hs], far[h], preferred_element_type=F32)
            o = attn[rows, hs]
            col = ecq[:, h : h + 1]
            for b in range(bits):
                at = h * levels + 5 + b
                gain = (lead * far_gain[b])[:, h : h + 1]
                o = o + (col * lwq[:, at : at + 1] * gain) * read[:, b * width : (b + 1) * width]
            mean_square = jnp.mean(o * o, axis=-1, keepdims=True)
            o = o * lax.rsqrt(mean_square + 1e-6) * gain_ref[h : h + 1, :]
            normed[pl.ds(pl.multiple_of(at_row, QUAD), QUAD), hs] = o.astype(BF16)

    def to_core(i, j):
        return pltpu.make_async_remote_copy(
            core_send.at[i, j], core_recv.at[i, j], cs_sem.at[i, j], cr_sem.at[i, j],
            device_id={"head": other_core}, device_id_type=MESH,
        )

    def to_chip(i, j):
        return pltpu.make_async_remote_copy(
            x_send.at[i, j], x_recv.at[i, j], xs_sem.at[i, j], xr_sem.at[i, j],
            device_id={"head": chip_of[i] * 2 + core}, device_id_type=MESH,
        )

    def product(which, j):
        rows = pl.ds(pl.multiple_of(which * block, block), block)
        cols = pl.ds(pl.multiple_of(j * piece_cols, piece_cols), piece_cols)
        return jnp.dot(normed[rows, :], w[:, cols], preferred_element_type=F32)

    per_group = group // QUAD
    for i in range(chips):

        @pl.loop(0, per_group)
        def _(n):
            finish_quad(chip_of[i] * per_group + n, n * QUAD)

        @pl.loop(0, PIECES + 1)
        def _(j):
            @pl.when(j < PIECES)
            def _():
                core_send[i, j] = product(1 - core, j).astype(BF16)
                to_core(i, j).start()

            @pl.when(j > 0)
            def _():
                mine = product(core, j - 1)
                to_core(i, j - 1).wait()
                mine = mine + core_recv[i, j - 1].astype(F32)
                if i < chips - 1:
                    x_send[i, j - 1] = mine.astype(BF16)
                    to_chip(i, j - 1).start()
                else:
                    acc[j - 1] = mine

    @pl.loop(0, PIECES)
    def _(j):
        mine = acc[j]
        for i in range(chips - 1):
            to_chip(i, j).wait()
            mine = mine + x_recv[i, j].astype(F32)
        cols = pl.ds(pl.multiple_of(j * piece_cols, piece_cols), piece_cols)
        out_ref[:, cols] = mine.astype(BF16)


def body(chips, bits, queries, keys, values, log_decay, level_weight, norm_gain, out_weight):
    rows, heads, width = queries.shape
    levels = level_weight.shape[2]
    depth, columns = out_weight.shape
    block = rows // (2 * chips)
    quads = rows // QUAD
    flat = (rows, heads * width)
    piece = (PIECES, block, columns // PIECES)
    decay = jnp.pad(log_decay, ((0, 0), (0, 128 - heads)))
    decay_t = jnp.transpose(log_decay.reshape(quads, QUAD, heads), (0, 2, 1))
    vmem = pl.BlockSpec(memory_space=pltpu.VMEM)
    hbm = pl.BlockSpec(memory_space=pl.ANY)
    dma = pltpu.SemaphoreType.DMA
    return pl.pallas_call(
        functools.partial(kernel, chips, bits, heads, levels, width),
        out_shape=jax.ShapeDtypeStruct((block, columns), BF16),
        in_specs=[hbm] * 4 + [vmem] * 4,
        out_specs=vmem,
        scratch_shapes=[
            pltpu.VMEM(flat, BF16),
            pltpu.VMEM(flat, BF16),
            pltpu.VMEM(flat, BF16),
            pltpu.VMEM((depth, columns), BF16),
            pltpu.VMEM((rows, 128), F32),
            pltpu.VMEM((quads, heads, QUAD), F32),
            pltpu.VMEM((quads, 8, 128), F32),
            pltpu.VMEM((quads, heads, width, width), F32),
            pltpu.VMEM((quads, heads, width, 2 * width), BF16),
            pltpu.VMEM(flat, F32),
            pltpu.VMEM((2 * block, heads * width), BF16),
            pltpu.VMEM((heads, width, width), F32),
            pltpu.VMEM((bits, heads, width, width), BF16),
            pltpu.VMEM((bits, heads, width, width), BF16),
            pltpu.VMEM((bits, 8, 128), F32),
            pltpu.VMEM((bits, 8, 128), F32),
            pltpu.VMEM((heads, width, bits * width), BF16),
            pltpu.VMEM((chips,) + piece, BF16),
            pltpu.VMEM((chips,) + piece, BF16),
            pltpu.VMEM((chips - 1,) + piece, BF16),
            pltpu.VMEM((chips - 1,) + piece, BF16),
            pltpu.VMEM(piece, F32),
            dma((4,)),
            dma((bits,)),
            dma((bits,)),
            dma((bits,)),
            dma((bits,)),
            dma((chips, PIECES)),
            dma((chips, PIECES)),
            dma((chips - 1, PIECES)),
            dma((chips - 1, PIECES)),
        ],
        compiler_params=pltpu.CompilerParams(
            collective_id=0, has_side_effects=True, vmem_limit_bytes=58 * 1024 * 1024
        ),
    )(
        queries.reshape(flat),
        keys.reshape(flat),
        values.reshape(flat),
        out_weight,
        decay,
        decay_t,
        level_weight.reshape(rows, heads * levels),
        norm_gain,
    )


def solution(mesh):
    chips = mesh.shape["head"] // 2
    bits = mesh.shape["seq"].bit_length() - 1
    return jax.shard_map(
        functools.partial(body, chips, bits),
        mesh=mesh,
        in_specs=(
            P("seq", "head", None),
            P("seq", "head", None),
            P("seq", "head", None),
            P("seq", "head"),
            P("seq", "head", None),
            P("head", None),
            P("head", None),
        ),
        out_specs=P(("seq", "head"), None),
        check_vma=False,
    )
```

time: 236 us -> 113 us (0.48)
  Pallas kernels: 0 us -> 99 us
  waiting for transfers between devices: 69.1 us -> 0 us
  matrix products: 61.1 us -> 0 us
  local copies, waits for them, and re-layouts: 54.1 us -> 13.3 us
  blocking collectives: 22.4 us -> 0 us
  other arithmetic: 14.4 us -> 0 us
  between operations: 13.8 us -> 0.02 us
    pallas_call x0 -> x1, Pallas kernels: none -> 99 us  [body(): pl.pallas_call(functools.partial(kernel, chips, bits, heads, levels, widt...]
    reduce_scatter x1 -> x0, waiting for transfers between devices: 69.1 us -> none  [body(): lax.psum_scatter(jnp.dot(normed, out_weight, preferred_element_type=jnp.f...]
    dot_general x9 -> x0, matrix products: 61.1 us -> none  [the longest x4 15.8 us: local_levels(): jnp.einsum('cthd,chde->cthe', query_blocks, picked, preferred_element_typ...]
    all_gather x1 -> x0, blocking collectives: 22.4 us -> none  [body(): all_totals = lax.all_gather(summary_total[None], 'seq', axis=0, tiled=True)]
    gather x13 -> x0, local copies, waits for them, and re-layouts: 21.9 us -> none  [the longest x4 18.8 us: local_levels(): picked = blocks[source].astype(jnp.bfloat16)]
    add x8 -> x0, local copies, waits for them, and re-layouts: 9.56 us -> none  [the longest x1 5.47 us: body(): output = output + jnp.sum(far_factor[:, :, :, :, None] * far_read, axis=2)]
    mul x7 -> x0, local copies, waits for them, and re-layouts: 7.21 us -> none  [the longest x4 5.05 us: local_levels(): output = output + factor[:, :, :, None] * readout]
    another operation x3 -> x0, other arithmetic: 6.39 us -> none  [the longest x1 6.33 us: body(): inner = jnp.cumsum(log_decay.reshape(span_count, SPAN, head_count), axis=1)]
  transfers between devices with their start and end apart: 2 -> 0, of which waited for: 1 -> 0; matrix products, arithmetic and copies ran while one was open for 26% -> 0% of each run, Pallas kernels for 0% -> 0%
where the time goes in v1:
time: 113 us; the launch traced here: 112 us
  Pallas kernels  99 us (88%)
  local copies, waits for them, and re-layouts  13.3 us (12%)
    pallas_call x1, Pallas kernels, body(): pl.pallas_call(functools.partial(kernel, chips, bits, heads, levels, widt...  99 us
    unnamed x9, local copies, waits for them, and re-layouts  7.06 us
    reshape x1, local copies, waits for them, and re-layouts, body(): values.reshape(flat)  3.25 us

profile of v1, /device:TPU:0, one launch (start us, length us, event | category | flops | bytes accessed | tf_op | source)
XLA Modules:
  0.0 112.3 jit_solution(11492657749242523999)
XLA Ops:
  0.0 0.0 copy-start
  0.0 2.1 %copy.11.lw_ref = f32[1024,64]{1,0:T(8,128)} copy(f32[1024,64]{0,1:T(8,128)} %bitcast.18) | data formatting | bytes 524288 | tf_op jit(solution)/shard_map/reshape | solution.py:329
  2.1 0.9 copy.10
  3.1 0.8 pad.4.ld_ref
  3.9 0.0 copy-done
  3.9 0.0 copy-start.1
  3.9 0.0 copy-start.2
  3.9 1.9 %copy.18 = bf16[128,8,8,128]{3,1,2,0:T(8,128)(2,1)} copy(bf16[128,8,8,128]{3,2,1,0:T(8,128)(2,1)S(1)} %bitcast.15) | data formatting | bytes 4194304
  5.9 0.0 copy-done.1
  5.9 1.0 copy-done.2
  6.9 3.3 %copy_bitcast_fusion = (bf16[1024,1024]{1,0:T(8,128)(2,1)}, bf16[1024,1024]{1,0:T(8,128)(2,1)}) fusion(bf16[128,8,8,128]{3,2,1,0:T(8,128)(2,1)S(1)} %bitcast.16, bf16[128,8,8,128]{3,2,1,0:T(8,128)(2,1)S(1)} %bitcast.17), kind=kLoop, calls=%fused_computation | loop fusion | bytes 8388608 | tf_op jit(solution)/shard_map/reshape | solution.py:325
  10.2 99.0 %shard_map.73 = bf16[256,4096]{1,0:T(8,128)(2,1)} custom-call(bf16[1024,1024]{1,0:T(8,128)(2,1)} %bitcast.14, bf16[1024,1024]{1,0:T(8,128)(2,1)} %get-tuple-element.6.k_hbm, bf16[1024,1024]{1,0:T(8,128)(2,1)} %get-tuple-element.5.v_hbm, bf16[1024,4096]{1,0:T(8,128)(2,1)} %w_hbm.1, f32[1024,128]{1,0:T(8,128)} %pad.4.ld_ref, f32[4,8,256]{2,1,0:T(8,128)} %bitcast.19, ...), custom_call_target="tpu_custom_call" | custom-call | tf_op jit(solution)/shard_map/pallas_call | solution.py:281
  109.2 3.1 %copy.20 = bf16[256,4096]{1,0:T(8,128)(2,1)} copy(bf16[256,4096]{1,0:T(8,128)(2,1)} %shard_map.73) | data formatting | bytes 4194304
Async XLA Ops:
  0.0 3.9 %copy-start = (bf16[1024,8,128]{2,1,0:T(8,128)(2,1)S(1)}, bf16[1024,8,128]{2,1,0:T(8,128)(2,1)}, u32[]{:S(2)}) copy-start(bf16[1024,8,128]{2,1,0:T(8,128)(2,1)} %param.7) | copy-start | bytes 6291460
  3.9 1.9 %copy-start.1 = (bf16[1024,8,128]{2,1,0:T(8,128)(2,1)S(1)}, bf16[1024,8,128]{2,1,0:T(8,128)(2,1)}, u32[]{:S(2)}) copy-start(bf16[1024,8,128]{2,1,0:T(8,128)(2,1)} %param.9) | copy-start | bytes 6291460
  3.9 3.0 %copy-start.2 = (bf16[1024,8,128]{2,1,0:T(8,128)(2,1)S(1)}, bf16[1024,8,128]{2,1,0:T(8,128)(2,1)}, u32[]{:S(2)}) copy-start(bf16[1024,8,128]{2,1,0:T(8,128)(2,1)} %param.8) | copy-start | bytes 6291460

commit v2 on v1

v2 whole, which is shorter than its diff:
```python
import functools

import jax
import jax.numpy as jnp
from jax import lax
from jax.experimental import pallas as pl
from jax.experimental.pallas import tpu as pltpu
from jax.sharding import PartitionSpec as P

SPAN = 64
QUAD = 4 * SPAN
PIECES = 4
PARTS = 4
F32 = jnp.float32
BF16 = jnp.bfloat16
HIGH = lax.Precision.HIGHEST
MESH = pl.DeviceIdType.MESH


def kernel(
    chips, bits, heads, levels, width,
    q_hbm, k_hbm, v_hbm, w_hbm, ldt_ref, lwt_ref, gain_ref, out_ref, x_recv,
    q, k, v, w, cum, cumt, lw_ref, tots, state, lev, attn, normed,
    summary, sum_send, sum_recv, tot_send, tot_recv, far,
    core_send, core_recv, x_send, acc,
    in_sem, ss_sem, sr_sem, ts_sem, tr_sem, cs_sem, cr_sem, xs_sem, xr_sem, out_sem,
):
    rows_all = q.shape[0]
    quads = rows_all // QUAD
    block = out_ref.shape[0]
    group = 2 * block
    piece_cols = out_ref.shape[1] // PIECES
    per_part = heads // PARTS
    position = lax.axis_index("seq")
    head_id = lax.axis_index("head")
    chip = head_id // 2
    core = head_id % 2
    other_core = chip * 2 + (1 - core)

    loads = [
        pltpu.make_async_copy(src, dst, in_sem.at[n])
        for n, (src, dst) in enumerate(((k_hbm, k), (v_hbm, v), (q_hbm, q), (w_hbm, w)))
    ]
    loads[0].start()
    loads[1].start()

    bit_of = [(position // (1 << b)) % 2 for b in range(bits)]
    partner_of = [position + (1 - 2 * bit_of[b]) * (1 << b) for b in range(bits)]
    chip_of = [(chip + 1 + i) % chips for i in range(chips)]

    barrier = pltpu.get_barrier_semaphore()
    for b in range(bits):
        pl.semaphore_signal(barrier, inc=1, device_id={"seq": partner_of[b]}, device_id_type=MESH)
    pl.semaphore_signal(barrier, inc=1, device_id={"head": other_core}, device_id_type=MESH)
    for i in range(chips - 1):
        pl.semaphore_signal(
            barrier, inc=1, device_id={"head": chip_of[i] * 2 + core}, device_id_type=MESH
        )
    pl.semaphore_wait(barrier, bits + chips)

    row_id = lax.broadcasted_iota(jnp.int32, (QUAD, QUAD), 0)
    col_id = lax.broadcasted_iota(jnp.int32, (QUAD, QUAD), 1)

    def head_cols(h):
        return slice(h * width, (h + 1) * width)

    def quad_rows(c):
        return pl.ds(pl.multiple_of(c * QUAD, QUAD), QUAD)

    @pl.loop(0, quads)
    def _(c):
        rows = quad_rows(c)
        lower = (row_id >= col_id).astype(F32)
        upper = (row_id <= col_id).astype(F32)
        decay = ldt_ref[:, rows]
        cumt[c] = jnp.dot(decay, upper, precision=HIGH, preferred_element_type=F32)
        wide = jnp.concatenate([decay, jnp.zeros((128 - heads, QUAD), F32)], axis=0)
        cq = lax.dot_general(
            lower, wide, (((1,), (1,)), ((), ())), precision=HIGH, preferred_element_type=F32
        )
        cum[rows, :] = cq
        tots[c] = jnp.broadcast_to(cq[QUAD - 1 : QUAD, :], (8, 128))
        lw_ref[rows, :] = jnp.transpose(lwt_ref[:, rows])

    t = [tots[c][0:1, :] for c in range(quads)]
    e1, e3, e23 = jnp.exp(t[1]), jnp.exp(t[3]), jnp.exp(t[2] + t[3])
    total = t[0] + t[1] + t[2] + t[3]
    before = [jnp.zeros_like(total), t[0], t[0] + t[1], t[0] + t[1] + t[2]]
    tot_send[0] = jnp.broadcast_to(total, (8, 128))

    def exchange_total(b):
        return pltpu.make_async_remote_copy(
            tot_send.at[b], tot_recv.at[b], ts_sem.at[b], tr_sem.at[b],
            device_id={"seq": partner_of[b]}, device_id_type=MESH,
        )

    def exchange(g, b):
        part = pl.ds(g * per_part, per_part)
        return pltpu.make_async_remote_copy(
            sum_send.at[b, part], sum_recv.at[b, part], ss_sem.at[b, g], sr_sem.at[b, g],
            device_id={"seq": partner_of[b]}, device_id_type=MESH,
        )

    exchange_total(0).start()
    loads[0].wait()
    loads[1].wait()
    loads[2].start()
    loads[3].start()

    nothing = jnp.zeros((width, width), BF16)
    for g in range(PARTS):
        members = range(g * per_part, (g + 1) * per_part)

        @pl.loop(0, quads)
        def _(c):
            rows = quad_rows(c)
            decay = jnp.exp(tots[c][0:1, :] - cum[rows, :])
            for h in members:
                hs = head_cols(h)
                scaled = (k[rows, hs].astype(F32) * decay[:, h : h + 1]).astype(BF16)
                state[c, h] = lax.dot_general(
                    scaled, v[rows, hs], (((0,), (0,)), ((), ())), preferred_element_type=F32
                )

        for h in members:
            s0, s2 = state[0, h], state[2, h]
            low = e1[:, h : h + 1] * s0 + state[1, h]
            whole = e23[:, h : h + 1] * low + e3[:, h : h + 1] * s2 + state[3, h]
            summary[h] = whole
            sum_send[0, h] = whole.astype(BF16)
            low_b = low.astype(BF16)
            lev[0, h, :, :width] = nothing
            lev[0, h, :, width:] = nothing
            lev[1, h, :, :width] = s0.astype(BF16)
            lev[1, h, :, width:] = nothing
            lev[2, h, :, :width] = nothing
            lev[2, h, :, width:] = low_b
            lev[3, h, :, :width] = s2.astype(BF16)
            lev[3, h, :, width:] = low_b
        exchange(g, 0).start()

    loads[2].wait()

    def local_quad(c, members):
        rows = quad_rows(c)
        cq = cum[rows, :]
        ecq = jnp.exp(cq)
        ct = cumt[c]
        lwq = lw_ref[rows, :]
        is_last = (c == quads - 1).astype(F32)
        g4 = is_last * jnp.exp(t[2]) + (1.0 - is_last)
        causal = row_id >= col_id
        same = (row_id // SPAN) == (col_id // SPAN)
        near = (row_id // (2 * SPAN)) == (col_id // (2 * SPAN))
        for h in members:
            hs = head_cols(h)
            at = h * levels
            qh = q[rows, hs]
            s = lax.dot_general(
                qh, k[rows, hs], (((1,), (1,)), ((), ())), preferred_element_type=F32
            )
            spread = jnp.where(causal, cq[:, h : h + 1] - ct[h : h + 1, :], -1e30)
            weight = jnp.where(
                same,
                lwq[:, at : at + 1],
                jnp.where(near, lwq[:, at + 1 : at + 2], lwq[:, at + 2 : at + 3]),
            )
            probs = (s * jnp.exp(spread) * weight).astype(BF16)
            o = jnp.dot(probs, v[rows, hs], preferred_element_type=F32)
            read = jnp.dot(qh, lev[c, h], preferred_element_type=F32)
            col = ecq[:, h : h + 1]
            o = o + (col * lwq[:, at + 3 : at + 4]) * read[:, :width]
            o = o + (col * lwq[:, at + 4 : at + 5] * g4[:, h : h + 1]) * read[:, width:]
            attn[rows, hs] = o

    far_gain, mine_by, other_by = [], [], []
    offset = jnp.zeros_like(total)
    turns = PARTS + bits - 1
    units = [(g, half) for g in range(PARTS) for half in range(2)]
    for turn in range(turns):
        for g, half in units[turn * len(units) // turns : (turn + 1) * len(units) // turns]:

            @pl.loop(half * quads // 2, (half + 1) * quads // 2)
            def _(c):
                local_quad(c, range(g * per_part, (g + 1) * per_part))

        for b in range(bits):
            g = turn - b
            if g < 0 or g >= PARTS:
                continue
            if g == 0:
                exchange_total(b).wait()
                flag = bit_of[b].astype(F32)
                other = tot_recv[b][0:1, :]
                far_gain.append(flag * jnp.exp(offset))
                mine_by.append(flag + (1.0 - flag) * jnp.exp(other))
                other_by.append(flag * jnp.exp(total) + (1.0 - flag))
                offset = offset + flag * other
                total = total + other
                if b < bits - 1:
                    tot_send[b + 1] = jnp.broadcast_to(total, (8, 128))
                    exchange_total(b + 1).start()
            exchange(g, b).wait()
            for h in range(g * per_part, (g + 1) * per_part):
                got = sum_recv[b, h]
                if b < bits - 1:
                    joint = (
                        mine_by[b][:, h : h + 1] * summary[h]
                        + other_by[b][:, h : h + 1] * got.astype(F32)
                    )
                    summary[h] = joint
                    sum_send[b + 1, h] = joint.astype(BF16)
                far[h, :, b * width : (b + 1) * width] = got
            if b < bits - 1:
                exchange(g, b + 1).start()

    loads[3].wait()

    def finish_quad(c, at_row):
        rows = quad_rows(c)
        ecq = jnp.exp(cum[rows, :])
        lwq = lw_ref[rows, :]
        lead = jnp.zeros_like(before[0])
        for n in range(1, quads):
            lead = lead + (c == n).astype(F32) * before[n]
        lead = jnp.exp(lead)
        for h in range(heads):
            hs = head_cols(h)
            read = jnp.dot(q[rows, hs], far[h], preferred_element_type=F32)
            o = attn[rows, hs]
            col = ecq[:, h : h + 1]
            for b in range(bits):
                at = h * levels + 5 + b
                gain = (lead * far_gain[b])[:, h : h + 1]
                o = o + (col * lwq[:, at : at + 1] * gain) * read[:, b * width : (b + 1) * width]
            mean_square = jnp.mean(o * o, axis=-1, keepdims=True)
            o = o * lax.rsqrt(mean_square + 1e-6) * gain_ref[h : h + 1, :]
            normed[pl.ds(pl.multiple_of(at_row, QUAD), QUAD), hs] = o.astype(BF16)

    def to_core(i, j):
        return pltpu.make_async_remote_copy(
            core_send.at[i, j], core_recv.at[i, j], cs_sem.at[i, j], cr_sem.at[i, j],
            device_id={"head": other_core}, device_id_type=MESH,
        )

    def piece(j):
        return pl.ds(pl.multiple_of(j * piece_cols, piece_cols), piece_cols)

    def to_chip(i, j):
        return pltpu.make_async_remote_copy(
            x_send.at[i, j], x_recv.at[i, :, piece(j)], xs_sem.at[i, j], xr_sem.at[i, j],
            device_id={"head": chip_of[i] * 2 + core}, device_id_type=MESH,
        )

    def to_out(j):
        return pltpu.make_async_copy(acc.at[j], out_ref.at[:, piece(j)], out_sem.at[j])

    def product(which, j):
        rows = pl.ds(pl.multiple_of(which * block, block), block)
        return jnp.dot(normed[rows, :], w[:, piece(j)], preferred_element_type=F32)

    per_group = group // QUAD
    for i in range(chips):

        @pl.loop(0, per_group)
        def _(n):
            finish_quad(chip_of[i] * per_group + n, n * QUAD)

        @pl.loop(0, PIECES + 1)
        def _(j):
            @pl.when(j < PIECES)
            def _():
                core_send[i, j] = product(1 - core, j).astype(BF16)
                to_core(i, j).start()

            @pl.when(j > 0)
            def _():
                mine = product(core, j - 1)
                to_core(i, j - 1).wait()
                mine = mine + core_recv[i, j - 1].astype(F32)
                if i < chips - 1:
                    x_send[i, j - 1] = mine.astype(BF16)
                    to_chip(i, j - 1).start()
                else:
                    acc[j - 1] = mine
                    to_out(j - 1).start()

    @pl.loop(0, PIECES)
    def _(j):
        to_out(j).wait()
        for i in range(chips - 1):
            to_chip(i, j).wait()


def body(chips, bits, queries, keys, values, log_decay, level_weight, norm_gain, out_weight):
    rows, heads, width = queries.shape
    levels = level_weight.shape[2]
    depth, columns = out_weight.shape
    block = rows // (2 * chips)
    quads = rows // QUAD
    flat = (rows, heads * width)
    piece = (PIECES, block, columns // PIECES)
    decay = jnp.transpose(log_decay)
    weights = jnp.transpose(level_weight, (1, 2, 0)).reshape(heads * levels, rows)
    vmem = pl.BlockSpec(memory_space=pltpu.VMEM)
    hbm = pl.BlockSpec(memory_space=pl.ANY)
    dma = pltpu.SemaphoreType.DMA
    mine, others = pl.pallas_call(
        functools.partial(kernel, chips, bits, heads, levels, width),
        out_shape=(
            jax.ShapeDtypeStruct((block, columns), F32),
            jax.ShapeDtypeStruct((chips - 1, block, columns), BF16),
        ),
        in_specs=[hbm] * 4 + [vmem] * 3,
        out_specs=(hbm, hbm),
        scratch_shapes=[
            pltpu.VMEM(flat, BF16),
            pltpu.VMEM(flat, BF16),
            pltpu.VMEM(flat, BF16),
            pltpu.VMEM((depth, columns), BF16),
            pltpu.VMEM((rows, 128), F32),
            pltpu.VMEM((quads, heads, QUAD), F32),
            pltpu.VMEM((rows, heads * levels), F32),
            pltpu.VMEM((quads, 8, 128), F32),
            pltpu.VMEM((quads, heads, width, width), F32),
            pltpu.VMEM((quads, heads, width, 2 * width), BF16),
            pltpu.VMEM(flat, F32),
            pltpu.VMEM((2 * block, heads * width), BF16),
            pltpu.VMEM((heads, width, width), F32),
            pltpu.VMEM((bits, heads, width, width), BF16),
            pltpu.VMEM((bits, heads, width, width), BF16),
            pltpu.VMEM((bits, 8, 128), F32),
            pltpu.VMEM((bits, 8, 128), F32),
            pltpu.VMEM((heads, width, bits * width), BF16),
            pltpu.VMEM((chips,) + piece, BF16),
            pltpu.VMEM((chips,) + piece, BF16),
            pltpu.VMEM((chips - 1,) + piece, BF16),
            pltpu.VMEM(piece, F32),
            dma((4,)),
            dma((bits, PARTS)),
            dma((bits, PARTS)),
            dma((bits,)),
            dma((bits,)),
            dma((chips, PIECES)),
            dma((chips, PIECES)),
            dma((chips - 1, PIECES)),
            dma((chips - 1, PIECES)),
            dma((PIECES,)),
        ],
        compiler_params=pltpu.CompilerParams(
            collective_id=0, has_side_effects=True, vmem_limit_bytes=58 * 1024 * 1024
        ),
    )(
        queries.reshape(flat),
        keys.reshape(flat),
        values.reshape(flat),
        out_weight,
        decay,
        weights,
        norm_gain,
    )
    for i in range(chips - 1):
        mine = mine + others[i].astype(F32)
    return mine.astype(BF16)


def solution(mesh):
    chips = mesh.shape["head"] // 2
    bits = mesh.shape["seq"].bit_length() - 1
    return jax.shard_map(
        functools.partial(body, chips, bits),
        mesh=mesh,
        in_specs=(
            P("seq", "head", None),
            P("seq", "head", None),
            P("seq", "head", None),
            P("seq", "head"),
            P("seq", "head", None),
            P("head", None),
            P("head", None),
        ),
        out_specs=P(("seq", "head"), None),
        check_vma=False,
    )
```

time: 113 us -> 104 us (0.920)
  Pallas kernels: 99 us -> 92 us
  local copies, waits for them, and re-layouts: 13.3 us -> 6.98 us
  other arithmetic: 0 us -> 4.75 us
    pallas_call x1, Pallas kernels: 99 us -> 92 us  [body(): pl.pallas_call(functools.partial(kernel, chips, bits, heads, levels, widt...]
    convert_element_type x0 -> x1, other arithmetic: none -> 4.75 us  [body(): return mine.astype(BF16)]
    unnamed x9 -> x5, local copies, waits for them, and re-layouts: 7.06 us -> 3.7 us
    reshape x1 -> x0, local copies, waits for them, and re-layouts: 2.11 us -> none  [body(): level_weight.reshape(rows, heads * levels)]
where the time goes in v2:
time: 104 us
  Pallas kernels  92 us (88%)
  local copies, waits for them, and re-layouts  6.98 us (7%)
  other arithmetic  4.75 us (5%)
    pallas_call x1, Pallas kernels, body(): pl.pallas_call(functools.partial(kernel, chips, bits, heads, levels, widt...  92 us
    convert_element_type x1, other arithmetic, body(): return mine.astype(BF16)  4.75 us
    unnamed x5, local copies, waits for them, and re-layouts  3.7 us
    reshape x1, local copies, waits for them, and re-layouts, body(): values.reshape(flat)  3.28 us

profile of v2, /device:TPU:0, one launch (start us, length us, event | category | flops | bytes accessed | tf_op | source)
XLA Modules:
  0.0 103.7 jit_solution(7127635251136361910)
XLA Ops:
  0.0 0.0 copy-start
  0.0 0.0 copy-start.1
  0.0 3.7 %copy.14 = bf16[128,8,8,128]{3,1,2,0:T(8,128)(2,1)} copy(bf16[128,8,8,128]{3,2,1,0:T(8,128)(2,1)} %bitcast.18) | data formatting | bytes 4194304
  3.7 0.0 copy-done
  3.7 0.0 copy-done.1
  3.7 3.3 %copy_bitcast_fusion = (bf16[1024,1024]{1,0:T(8,128)(2,1)}, bf16[1024,1024]{1,0:T(8,128)(2,1)}) fusion(bf16[128,8,8,128]{3,2,1,0:T(8,128)(2,1)S(1)} %bitcast.19, bf16[128,8,8,128]{3,2,1,0:T(8,128)(2,1)S(1)} %bitcast.20), kind=kLoop, calls=%fused_computation.2 | loop fusion | bytes 8388608 | tf_op jit(solution)/shard_map/reshape | solution.py:356
  7.0 92.0 %shard_map.73 = (f32[256,4096]{1,0:T(8,128)}, bf16[1,256,4096]{2,1,0:T(8,128)(2,1)}) custom-call(bf16[1024,1024]{1,0:T(8,128)(2,1)} %bitcast.17, bf16[1024,1024]{1,0:T(8,128)(2,1)} %get-tuple-element.10.k_hbm, bf16[1024,1024]{1,0:T(8,128)(2,1)} %get-tuple-element.9.v_hbm, bf16[1024,4096]{1,0:T(8,128)(2,1)} %w_hbm.1, f32[8,1024]{1,0:T(8,128)} %bitcast.22, ...), custom_call_target="tpu_custom_call" | custom-call | tf_op jit(solution)/shard_map/pallas_call | solution.py:308
  99.0 4.7 %fusion = bf16[256,4096]{1,0:T(8,128)(2,1)} fusion(f32[256,4096]{1,0:T(8,128)} %get-tuple-element.7, bf16[1,256,4096]{2,1,0:T(8,128)(2,1)} %get-tuple-element.8), kind=kLoop, calls=%fused_computation.1 | loop fusion | flops 3145728 | bytes 8388608 | tf_op jit(solution)/shard_map/convert_element_type | solution.py:364
Async XLA Ops:
  0.0 3.7 %copy-start = (bf16[1024,8,128]{2,1,0:T(8,128)(2,1)S(1)}, bf16[1024,8,128]{2,1,0:T(8,128)(2,1)}, u32[]{:S(2)}) copy-start(bf16[1024,8,128]{2,1,0:T(8,128)(2,1)} %param.9) | copy-start | bytes 6291460
  0.0 3.7 %copy-start.1 = (bf16[1024,8,128]{2,1,0:T(8,128)(2,1)S(1)}, bf16[1024,8,128]{2,1,0:T(8,128)(2,1)}, u32[]{:S(2)}) copy-start(bf16[1024,8,128]{2,1,0:T(8,128)(2,1)} %param.8) | copy-start | bytes 6291460

commit v3 on v2

--- a/solution.py
+++ b/solution.py
@@ -67,6 +67,17 @@
     def quad_rows(c):
         return pl.ds(pl.multiple_of(c * QUAD, QUAD), QUAD)
 
+    def lane_head(ids):
+        return sum((ids >= h * levels).astype(jnp.int32) for h in range(1, heads))
+
+    def lane(h):
+        return slice(h * levels, h * levels + 1)
+
+    lane_id = lax.broadcasted_iota(jnp.int32, (1, 128), 1)
+    level_id = lane_id - levels * lane_head(lane_id)
+    spread_head = lane_head(lax.broadcasted_iota(jnp.int32, (128, heads), 0))
+    spread = (spread_head == lax.broadcasted_iota(jnp.int32, (128, heads), 1)).astype(F32)
+
     @pl.loop(0, quads)
     def _(c):
         rows = quad_rows(c)
@@ -74,13 +85,15 @@
         upper = (row_id <= col_id).astype(F32)
         decay = ldt_ref[:, rows]
         cumt[c] = jnp.dot(decay, upper, precision=HIGH, preferred_element_type=F32)
-        wide = jnp.concatenate([decay, jnp.zeros((128 - heads, QUAD), F32)], axis=0)
+        wide = jnp.dot(spread, decay, precision=HIGH, preferred_element_type=F32)
         cq = lax.dot_general(
             lower, wide, (((1,), (1,)), ((), ())), precision=HIGH, preferred_element_type=F32
         )
         cum[rows, :] = cq
         tots[c] = jnp.broadcast_to(cq[QUAD - 1 : QUAD, :], (8, 128))
-        lw_ref[rows, :] = jnp.transpose(lwt_ref[:, rows])
+        padding = jnp.zeros((128 - heads * levels, QUAD), F32)
+        weights = jnp.transpose(jnp.concatenate([lwt_ref[:, rows], padding], axis=0))
+        lw_ref[rows, :] = weights * jnp.where(level_id >= 3, jnp.exp(cq), 1.0)
 
     t = [tots[c][0:1, :] for c in range(quads)]
     e1, e3, e23 = jnp.exp(t[1]), jnp.exp(t[3]), jnp.exp(t[2] + t[3])
@@ -117,15 +130,15 @@
             decay = jnp.exp(tots[c][0:1, :] - cum[rows, :])
             for h in members:
                 hs = head_cols(h)
-                scaled = (k[rows, hs].astype(F32) * decay[:, h : h + 1]).astype(BF16)
+                scaled = (k[rows, hs].astype(F32) * decay[:, lane(h)]).astype(BF16)
                 state[c, h] = lax.dot_general(
                     scaled, v[rows, hs], (((0,), (0,)), ((), ())), preferred_element_type=F32
                 )
 
         for h in members:
             s0, s2 = state[0, h], state[2, h]
-            low = e1[:, h : h + 1] * s0 + state[1, h]
-            whole = e23[:, h : h + 1] * low + e3[:, h : h + 1] * s2 + state[3, h]
+            low = e1[:, lane(h)] * s0 + state[1, h]
+            whole = e23[:, lane(h)] * low + e3[:, lane(h)] * s2 + state[3, h]
             summary[h] = whole
             sum_send[0, h] = whole.astype(BF16)
             low_b = low.astype(BF16)
@@ -141,37 +154,49 @@
 
     loads[2].wait()
 
+    strip_row = lax.broadcasted_iota(jnp.int32, (SPAN, 2 * SPAN), 0)
+    strip_col = lax.broadcasted_iota(jnp.int32, (SPAN, 2 * SPAN), 1)
+
     def local_quad(c, members):
-        rows = quad_rows(c)
-        cq = cum[rows, :]
-        ecq = jnp.exp(cq)
+        base = c * QUAD
         ct = cumt[c]
-        lwq = lw_ref[rows, :]
         is_last = (c == quads - 1).astype(F32)
-        g4 = is_last * jnp.exp(t[2]) + (1.0 - is_last)
-        causal = row_id >= col_id
-        same = (row_id // SPAN) == (col_id // SPAN)
-        near = (row_id // (2 * SPAN)) == (col_id // (2 * SPAN))
-        for h in members:
-            hs = head_cols(h)
-            at = h * levels
-            qh = q[rows, hs]
-            s = lax.dot_general(
-                qh, k[rows, hs], (((1,), (1,)), ((), ())), preferred_element_type=F32
-            )
-            spread = jnp.where(causal, cq[:, h : h + 1] - ct[h : h + 1, :], -1e30)
-            weight = jnp.where(
-                same,
-                lwq[:, at : at + 1],
-                jnp.where(near, lwq[:, at + 1 : at + 2], lwq[:, at + 2 : at + 3]),
-            )
-            probs = (s * jnp.exp(spread) * weight).astype(BF16)
-            o = jnp.dot(probs, v[rows, hs], preferred_element_type=F32)
-            read = jnp.dot(qh, lev[c, h], preferred_element_type=F32)
-            col = ecq[:, h : h + 1]
-            o = o + (col * lwq[:, at + 3 : at + 4]) * read[:, :width]
-            o = o + (col * lwq[:, at + 4 : at + 5] * g4[:, h : h + 1]) * read[:, width:]
-            attn[rows, hs] = o
+        g4 = jnp.where(level_id == 4, is_last * jnp.exp(t[2]) + (1.0 - is_last), 1.0)
+        for side in range(2):
+            rows = pl.ds(pl.multiple_of(base + side * 2 * SPAN, 2 * SPAN), 2 * SPAN)
+            seen = pl.ds(pl.multiple_of(base, QUAD), (side + 1) * 2 * SPAN)
+            cq = cum[rows, :]
+            fq = lw_ref[rows, :] * g4
+            for h in members:
+                hs = head_cols(h)
+                at = h * levels
+                qh = q[rows, hs]
+                s = lax.dot_general(
+                    qh, k[seen, hs], (((1,), (1,)), ((), ())), preferred_element_type=F32
+                )
+                strips = []
+                for n in range(2):
+                    top = slice(n * SPAN, (n + 1) * SPAN)
+                    col = cq[top, lane(h)]
+                    own = fq[top, at : at + 1]
+                    if n == 1:
+                        own = jnp.where(strip_col < SPAN, fq[top, at + 1 : at + 2], own)
+                    diag = slice(side * 2 * SPAN, (side + 1) * 2 * SPAN)
+                    gap = jnp.where(
+                        strip_row + n * SPAN >= strip_col, col - ct[h : h + 1, diag], -1e30
+                    )
+                    strip = (s[top, diag] * (jnp.exp(gap) * own)).astype(BF16)
+                    if side == 1:
+                        gap = col - ct[h : h + 1, : 2 * SPAN]
+                        far_side = s[top, : 2 * SPAN] * (jnp.exp(gap) * fq[top, at + 2 : at + 3])
+                        strip = jnp.concatenate([far_side.astype(BF16), strip], axis=1)
+                    strips.append(strip)
+                probs = jnp.concatenate(strips, axis=0)
+                o = jnp.dot(probs, v[seen, hs], preferred_element_type=F32)
+                read = jnp.dot(qh, lev[c, h], preferred_element_type=F32)
+                o = o + fq[:, at + 3 : at + 4] * read[:, :width]
+                o = o + fq[:, at + 4 : at + 5] * read[:, width:]
+                attn[rows, hs] = o
 
     far_gain, mine_by, other_by = [], [], []
     offset = jnp.zeros_like(total)
@@ -205,8 +230,8 @@
                 got = sum_recv[b, h]
                 if b < bits - 1:
                     joint = (
-                        mine_by[b][:, h : h + 1] * summary[h]
-                        + other_by[b][:, h : h + 1] * got.astype(F32)
+                        mine_by[b][:, lane(h)] * summary[h]
+                        + other_by[b][:, lane(h)] * got.astype(F32)
                     )
                     summary[h] = joint
                     sum_send[b + 1, h] = joint.astype(BF16)
@@ -216,26 +241,30 @@
 
     loads[3].wait()
 
+    reach = jnp.ones((1, 128), F32)
+    for b in range(bits):
+        reach = jnp.where(level_id == 5 + b, far_gain[b], reach)
+
     def finish_quad(c, at_row):
-        rows = quad_rows(c)
-        ecq = jnp.exp(cum[rows, :])
-        lwq = lw_ref[rows, :]
         lead = jnp.zeros_like(before[0])
         for n in range(1, quads):
             lead = lead + (c == n).astype(F32) * before[n]
-        lead = jnp.exp(lead)
-        for h in range(heads):
-            hs = head_cols(h)
-            read = jnp.dot(q[rows, hs], far[h], preferred_element_type=F32)
-            o = attn[rows, hs]
-            col = ecq[:, h : h + 1]
-            for b in range(bits):
-                at = h * levels + 5 + b
-                gain = (lead * far_gain[b])[:, h : h + 1]
-                o = o + (col * lwq[:, at : at + 1] * gain) * read[:, b * width : (b + 1) * width]
-            mean_square = jnp.mean(o * o, axis=-1, keepdims=True)
-            o = o * lax.rsqrt(mean_square + 1e-6) * gain_ref[h : h + 1, :]
-            normed[pl.ds(pl.multiple_of(at_row, QUAD), QUAD), hs] = o.astype(BF16)
+        gain = reach * jnp.exp(lead)
+        for side in range(2):
+            skip = side * 2 * SPAN
+            rows = pl.ds(pl.multiple_of(c * QUAD + skip, 2 * SPAN), 2 * SPAN)
+            into = pl.ds(pl.multiple_of(at_row + skip, 2 * SPAN), 2 * SPAN)
+            fq = lw_ref[rows, :] * gain
+            for h in range(heads):
+                hs = head_cols(h)
+                read = jnp.dot(q[rows, hs], far[h], preferred_element_type=F32)
+                o = attn[rows, hs]
+                for b in range(bits):
+                    at = h * levels + 5 + b
+                    o = o + fq[:, at : at + 1] * read[:, b * width : (b + 1) * width]
+                mean_square = jnp.mean(o * o, axis=-1, keepdims=True)
+                o = o * lax.rsqrt(mean_square + 1e-6) * gain_ref[h : h + 1, :]
+                normed[into, hs] = o.astype(BF16)
 
     def to_core(i, j):
         return pltpu.make_async_remote_copy(
@@ -282,7 +311,7 @@
                     x_send[i, j - 1] = mine.astype(BF16)
                     to_chip(i, j - 1).start()
                 else:
-                    acc[j - 1] = mine
+                    acc[j - 1] = mine.astype(BF16)
                     to_out(j - 1).start()
 
     @pl.loop(0, PIECES)
@@ -308,7 +337,7 @@
     mine, others = pl.pallas_call(
         functools.partial(kernel, chips, bits, heads, levels, width),
         out_shape=(
-            jax.ShapeDtypeStruct((block, columns), F32),
+            jax.ShapeDtypeStruct((block, columns), BF16),
             jax.ShapeDtypeStruct((chips - 1, block, columns), BF16),
         ),
         in_specs=[hbm] * 4 + [vmem] * 3,
@@ -320,7 +349,7 @@
             pltpu.VMEM((depth, columns), BF16),
             pltpu.VMEM((rows, 128), F32),
             pltpu.VMEM((quads, heads, QUAD), F32),
-            pltpu.VMEM((rows, heads * levels), F32),
+            pltpu.VMEM((rows, 128), F32),
             pltpu.VMEM((quads, 8, 128), F32),
             pltpu.VMEM((quads, heads, width, width), F32),
             pltpu.VMEM((quads, heads, width, 2 * width), BF16),
@@ -335,7 +364,7 @@
             pltpu.VMEM((chips,) + piece, BF16),
             pltpu.VMEM((chips,) + piece, BF16),
             pltpu.VMEM((chips - 1,) + piece, BF16),
-            pltpu.VMEM(piece, F32),
+            pltpu.VMEM(piece, BF16),
             dma((4,)),
             dma((bits, PARTS)),
             dma((bits, PARTS)),
@@ -359,6 +388,7 @@
         weights,
         norm_gain,
     )
+    mine = mine.astype(F32)
     for i in range(chips - 1):
         mine = mine + others[i].astype(F32)
     return mine.astype(BF16)

time: 104 us -> 100 us (0.962)
  Pallas kernels: 92 us -> 88.9 us
    pallas_call x1, Pallas kernels: 92 us -> 88.9 us  [body(): pl.pallas_call(functools.partial(kernel, chips, bits, heads, levels, widt...]
where the time goes in v3:
time: 100 us
  Pallas kernels  88.9 us (89%)
  local copies, waits for them, and re-layouts  6.96 us (7%)
  other arithmetic  4.33 us (4%)
    pallas_call x1, Pallas kernels, body(): pl.pallas_call(functools.partial(kernel, chips, bits, heads, levels, widt...  88.9 us
    convert_element_type x1, other arithmetic, body(): return mine.astype(BF16)  4.33 us
    unnamed x5, local copies, waits for them, and re-layouts  3.7 us
    reshape x1, local copies, waits for them, and re-layouts, body(): values.reshape(flat)  3.26 us

profile of v3, /device:TPU:0, one launch (start us, length us, event | category | flops | bytes accessed | tf_op | source)
XLA Modules:
  0.0 100.2 jit_solution(2757326139527366249)
XLA Ops:
  0.0 0.0 copy-start
  0.0 0.0 copy-start.1
  0.0 3.7 %copy.14 = bf16[128,8,8,128]{3,1,2,0:T(8,128)(2,1)} copy(bf16[128,8,8,128]{3,2,1,0:T(8,128)(2,1)} %bitcast.18) | data formatting | bytes 4194304
  3.7 0.0 copy-done
  3.7 0.0 copy-done.1
  3.7 3.3 %copy_bitcast_fusion = (bf16[1024,1024]{1,0:T(8,128)(2,1)}, bf16[1024,1024]{1,0:T(8,128)(2,1)}) fusion(bf16[128,8,8,128]{3,2,1,0:T(8,128)(2,1)S(1)} %bitcast.19, bf16[128,8,8,128]{3,2,1,0:T(8,128)(2,1)S(1)} %bitcast.20), kind=kLoop, calls=%fused_computation.2 | loop fusion | bytes 8388608 | tf_op jit(solution)/shard_map/reshape | solution.py:385
  7.0 88.9 %shard_map.73 = (bf16[256,4096]{1,0:T(8,128)(2,1)}, bf16[1,256,4096]{2,1,0:T(8,128)(2,1)}) custom-call(bf16[1024,1024]{1,0:T(8,128)(2,1)} %bitcast.17, bf16[1024,1024]{1,0:T(8,128)(2,1)} %get-tuple-element.10.k_hbm, bf16[1024,1024]{1,0:T(8,128)(2,1)} %get-tuple-element.9.v_hbm, bf16[1024,4096]{1,0:T(8,128)(2,1)} %w_hbm.1, f32[8,1024]{1,0:T(8,128)} %bitcast.22, ...), custom_call_target="tpu_custom_call" | custom-call | tf_op jit(solution)/shard_map/pallas_call | solution.py:337
  95.8 4.3 %fusion = bf16[256,4096]{1,0:T(8,128)(2,1)} fusion(bf16[256,4096]{1,0:T(8,128)(2,1)} %get-tuple-element.7, bf16[1,256,4096]{2,1,0:T(8,128)(2,1)} %get-tuple-element.8), kind=kLoop, calls=%fused_computation.1 | loop fusion | flops 4194304 | bytes 6291456 | tf_op jit(solution)/shard_map/convert_element_type | solution.py:394
Async XLA Ops:
  0.0 3.7 %copy-start = (bf16[1024,8,128]{2,1,0:T(8,128)(2,1)S(1)}, bf16[1024,8,128]{2,1,0:T(8,128)(2,1)}, u32[]{:S(2)}) copy-start(bf16[1024,8,128]{2,1,0:T(8,128)(2,1)} %param.9) | copy-start | bytes 6291460
  0.0 3.7 %copy-start.1 = (bf16[1024,8,128]{2,1,0:T(8,128)(2,1)S(1)}, bf16[1024,8,128]{2,1,0:T(8,128)(2,1)}, u32[]{:S(2)}) copy-start(bf16[1024,8,128]{2,1,0:T(8,128)(2,1)} %param.8) | copy-start | bytes 6291460

commit v4 on v3

--- a/solution.py
+++ b/solution.py
@@ -45,18 +45,34 @@
     loads[1].start()
 
     bit_of = [(position // (1 << b)) % 2 for b in range(bits)]
-    partner_of = [position + (1 - 2 * bit_of[b]) * (1 << b) for b in range(bits)]
+    partner_of = [position + (1 - 2 * bit_of[b]) * (1 << b) for b in range(bits - 1)]
+    row = 1 << (bits // 2)
+    half = 1 << (bits - 1)
+    gives = (position >= half - row) & (position < 2 * half - row)
+    takes = position >= half
+    above = (position + row) % (2 * half)
+    below = (position - row + 2 * half) % (2 * half)
     chip_of = [(chip + 1 + i) % chips for i in range(chips)]
 
     barrier = pltpu.get_barrier_semaphore()
-    for b in range(bits):
+    for b in range(bits - 1):
         pl.semaphore_signal(barrier, inc=1, device_id={"seq": partner_of[b]}, device_id_type=MESH)
+
+    @pl.when(gives)
+    def _():
+        pl.semaphore_signal(barrier, inc=1, device_id={"seq": above}, device_id_type=MESH)
+
+    @pl.when(takes)
+    def _():
+        pl.semaphore_signal(barrier, inc=1, device_id={"seq": below}, device_id_type=MESH)
+
     pl.semaphore_signal(barrier, inc=1, device_id={"head": other_core}, device_id_type=MESH)
     for i in range(chips - 1):
         pl.semaphore_signal(
             barrier, inc=1, device_id={"head": chip_of[i] * 2 + core}, device_id_type=MESH
         )
-    pl.semaphore_wait(barrier, bits + chips)
+    chained = position // half + ((position + row) // half) % 2
+    pl.semaphore_wait(barrier, bits - 1 + chips + chained)
 
     row_id = lax.broadcasted_iota(jnp.int32, (QUAD, QUAD), 0)
     col_id = lax.broadcasted_iota(jnp.int32, (QUAD, QUAD), 1)
@@ -112,6 +128,14 @@
         return pltpu.make_async_remote_copy(
             sum_send.at[b, part], sum_recv.at[b, part], ss_sem.at[b, g], sr_sem.at[b, g],
             device_id={"seq": partner_of[b]}, device_id_type=MESH,
+        )
+
+    def hand_on(g, src):
+        part = pl.ds(g * per_part, per_part)
+        b = bits - 1
+        return pltpu.make_async_remote_copy(
+            src.at[b, part], sum_recv.at[b, part], ss_sem.at[b, g], sr_sem.at[b, g],
+            device_id={"seq": above}, device_id_type=MESH,
         )
 
     exchange_total(0).start()
@@ -199,17 +223,18 @@
                 attn[rows, hs] = o
 
     far_gain, mine_by, other_by = [], [], []
+    top = bits - 1
     offset = jnp.zeros_like(total)
-    turns = PARTS + bits - 1
-    units = [(g, half) for g in range(PARTS) for half in range(2)]
+    turns = PARTS + bits
+    units = [(g, end) for g in range(PARTS) for end in range(2)]
     for turn in range(turns):
-        for g, half in units[turn * len(units) // turns : (turn + 1) * len(units) // turns]:
-
-            @pl.loop(half * quads // 2, (half + 1) * quads // 2)
+        for g, end in units[turn * len(units) // turns : (turn + 1) * len(units) // turns]:
+
+            @pl.loop(end * quads // 2, (end + 1) * quads // 2)
             def _(c):
                 local_quad(c, range(g * per_part, (g + 1) * per_part))
 
-        for b in range(bits):
+        for b in range(top):
             g = turn - b
             if g < 0 or g >= PARTS:
                 continue
@@ -222,22 +247,54 @@
                 other_by.append(flag * jnp.exp(total) + (1.0 - flag))
                 offset = offset + flag * other
                 total = total + other
-                if b < bits - 1:
+                if b < top - 1:
                     tot_send[b + 1] = jnp.broadcast_to(total, (8, 128))
                     exchange_total(b + 1).start()
             exchange(g, b).wait()
             for h in range(g * per_part, (g + 1) * per_part):
                 got = sum_recv[b, h]
-                if b < bits - 1:
-                    joint = (
-                        mine_by[b][:, lane(h)] * summary[h]
-                        + other_by[b][:, lane(h)] * got.astype(F32)
-                    )
-                    summary[h] = joint
-                    sum_send[b + 1, h] = joint.astype(BF16)
+                joint = (
+                    mine_by[b][:, lane(h)] * summary[h]
+                    + other_by[b][:, lane(h)] * got.astype(F32)
+                )
+                summary[h] = joint
+                sum_send[b + 1, h] = joint.astype(BF16)
                 far[h, :, b * width : (b + 1) * width] = got
-            if b < bits - 1:
+            if b < top - 1:
                 exchange(g, b + 1).start()
+            else:
+
+                @pl.when(gives & (position < half))
+                def _():
+                    hand_on(g, sum_send).start()
+
+        g = turn - bits
+        if g >= 0:
+
+            @pl.when(takes)
+            def _():
+                hand_on(g, sum_recv).wait_recv()
+
+            @pl.when(takes & gives)
+            def _():
+                hand_on(g, sum_recv).start()
+
+            for h in range(g * per_part, (g + 1) * per_part):
+
+                @pl.when(takes)
+                def _():
+                    far[h, :, top * width :] = sum_recv[top, h]
+
+                @pl.when(position < half)
+                def _():
+                    far[h, :, top * width :] = nothing
+
+    far_gain.append(bit_of[top].astype(F32) * jnp.exp(offset))
+
+    @pl.when(gives)
+    def _():
+        for g in range(PARTS):
+            hand_on(g, sum_send).wait_send()
 
     loads[3].wait()
 

time: 100 us -> 97.8 us (0.978)
  the two profiles are of different devices: /device:TPU:0 before, /device:TPU:24 now
where the time goes in v4:
time: 97.8 us; the launch traced here: 97.6 us
  Pallas kernels  86.3 us (88%)
  local copies, waits for them, and re-layouts  6.96 us (7%)
  other arithmetic  4.33 us (4%)
    pallas_call x1, Pallas kernels, body(): pl.pallas_call(functools.partial(kernel, chips, bits, heads, levels, widt...  86.3 us
    convert_element_type x1, other arithmetic, body(): return mine.astype(BF16)  4.33 us
    unnamed x5, local copies, waits for them, and re-layouts  3.7 us
    reshape x1, local copies, waits for them, and re-layouts, body(): values.reshape(flat)  3.26 us

profile of v4, /device:TPU:24, one launch (start us, length us, event | category | flops | bytes accessed | tf_op | source)
XLA Modules:
  0.0 97.6 jit_solution(12444972170113441624)
XLA Ops:
  0.0 0.0 copy-start
  0.0 0.0 copy-start.1
  0.0 3.7 %copy.14 = bf16[128,8,8,128]{3,1,2,0:T(8,128)(2,1)} copy(bf16[128,8,8,128]{3,2,1,0:T(8,128)(2,1)} %bitcast.18) | data formatting | bytes 4194304
  3.7 0.0 copy-done
  3.7 0.0 copy-done.1
  3.7 3.3 %copy_bitcast_fusion = (bf16[1024,1024]{1,0:T(8,128)(2,1)}, bf16[1024,1024]{1,0:T(8,128)(2,1)}) fusion(bf16[128,8,8,128]{3,2,1,0:T(8,128)(2,1)S(1)} %bitcast.19, bf16[128,8,8,128]{3,2,1,0:T(8,128)(2,1)S(1)} %bitcast.20), kind=kLoop, calls=%fused_computation.2 | loop fusion | bytes 8388608 | tf_op jit(solution)/shard_map/reshape | solution.py:442
  7.0 86.3 %shard_map.73 = (bf16[256,4096]{1,0:T(8,128)(2,1)}, bf16[1,256,4096]{2,1,0:T(8,128)(2,1)}) custom-call(bf16[1024,1024]{1,0:T(8,128)(2,1)} %bitcast.17, bf16[1024,1024]{1,0:T(8,128)(2,1)} %get-tuple-element.10.k_hbm, bf16[1024,1024]{1,0:T(8,128)(2,1)} %get-tuple-element.9.v_hbm, bf16[1024,4096]{1,0:T(8,128)(2,1)} %w_hbm.1, f32[8,1024]{1,0:T(8,128)} %bitcast.22, ...), custom_call_target="tpu_custom_call" | custom-call | tf_op jit(solution)/shard_map/pallas_call | solution.py:394
  93.3 4.3 %fusion = bf16[256,4096]{1,0:T(8,128)(2,1)} fusion(bf16[256,4096]{1,0:T(8,128)(2,1)} %get-tuple-element.7, bf16[1,256,4096]{2,1,0:T(8,128)(2,1)} %get-tuple-element.8), kind=kLoop, calls=%fused_computation.1 | loop fusion | flops 4194304 | bytes 6291456 | tf_op jit(solution)/shard_map/convert_element_type | solution.py:451
Async XLA Ops:
  0.0 3.7 %copy-start = (bf16[1024,8,128]{2,1,0:T(8,128)(2,1)S(1)}, bf16[1024,8,128]{2,1,0:T(8,128)(2,1)}, u32[]{:S(2)}) copy-start(bf16[1024,8,128]{2,1,0:T(8,128)(2,1)} %param.9) | copy-start | bytes 6291460
  0.0 3.7 %copy-start.1 = (bf16[1024,8,128]{2,1,0:T(8,128)(2,1)S(1)}, bf16[1024,8,128]{2,1,0:T(8,128)(2,1)}, u32[]{:S(2)}) copy-start(bf16[1024,8,128]{2,1,0:T(8,128)(2,1)} %param.8) | copy-start | bytes 6291460
